TPU v7x, 512 devices: a whole 4x4x16 slice. The times are simulated.
512 devices in a mesh: shot: 8 (over z_lo), slab: 64 (over x, z_hi, y, core).
Axes of the slice: x: 4, y: 4, z: 16 (z_hi: 2, z_lo: 8; z = z_hi * 8 + z_lo), core: 2. Of those that a mesh axis runs over, the one named last changes fastest.
Arguments:
- partial_grads: bfloat16 [8, 3, 1024, 128, 256], P('shot', None, 'slab'), may hold values from -6 to 6
- model: float32 [3, 1024, 128, 256], P(None, 'slab', 'shot'), may hold values from 0.8 to 1.6
- tilt: float32 [1024, 128, 256], P('slab', 'shot'), may hold values from -3.140625 to 3.140625
- widths: float32 [3, 1024], replicated, may hold values from 2 to 64
- step_length: float32 [3], replicated, may hold values from 0.1 to 0.4
Outputs:
- coefficients: float32 [3, 1024, 128, 256], P(None, 'slab', 'shot')
All inputs are finite; a program needn't handle non-finite values.
Results may differ from a plain program's by a relative error of at most 0.004.
Values may be sent and summed in bfloat16 or wider, within the bound.
A program may use at most 64 MiB of HBM per device.

v0:
```python
import jax
import jax.numpy as jnp
from jax import lax
from jax.sharding import Mesh
from jax.sharding import PartitionSpec as P

SLAB = ("slab_0", "slab_1", "slab_2", "slab_3")


def in_blocks(x, dim, length):
    lengths = x.shape
    parts = x.reshape(*lengths[:dim], length, lengths[dim] // length, *lengths[dim + 1 :])
    return jnp.moveaxis(parts, dim, 0)


def in_order(parts, dim):
    lengths = list(parts.shape[1:])
    lengths[dim] *= parts.shape[0]
    return jnp.moveaxis(parts, 0, dim).reshape(lengths)


def moved_by_axis(parts, axes, sequence):
    inside = parts.shape[1:]
    filled = parts.reshape(*(lax.axis_size(a) for a in axes), *inside)
    for k in sequence:
        filled = lax.all_to_all(filled, axes[k], k, k, tiled=True)
    return filled.reshape(-1, *inside)


def exchange_by_chip(x, groups, sequence, split_dim, concat_dim):
    length = lax.axis_size(groups[0]) * lax.axis_size(groups[1])
    parts = in_blocks(x, split_dim, length)
    return in_order(moved_by_axis(parts, groups, sequence), concat_dim)


def padded_2(block, sides, width):
    for axis, dim in sides:
        count = lax.axis_size(axis)
        forward = [(i, i + 1) for i in range(count - 1)]
        backward = [(target, source) for source, target in forward]
        low = lax.ppermute(
            lax.slice_in_dim(block, block.shape[dim] - width, None, axis=dim), axis, forward
        )
        high = lax.ppermute(lax.slice_in_dim(block, 0, width, axis=dim), axis, backward)
        block = jnp.concatenate([low, block, high], axis=dim)
    return block


def smoother(width_row):
    depth_count = width_row.shape[0]
    depths = jnp.arange(depth_count, dtype=jnp.float32)
    offset = depths[:, None] - depths[None, :]
    kernel = jnp.exp(-offset * offset / (2.0 * width_row[:, None] * width_row[:, None]))
    return (kernel / jnp.sum(kernel, axis=1, keepdims=True)).astype(jnp.bfloat16)


def rotate(velocity, epsilon, delta, angle):
    squared = velocity * velocity
    along = squared * (1.0 + 2.0 * epsilon)
    normal = squared * (1.0 + 2.0 * delta)
    cosine = jnp.cos(angle)
    sine = jnp.sin(angle)
    first = along * cosine * cosine + squared * sine * sine
    second = along * sine * sine + squared * cosine * cosine
    third = (normal - squared) * sine * cosine
    return jnp.stack([first, second, third])


def average(padded):
    depth_cells = padded.shape[1] - 2
    x_cells = padded.shape[2] - 2
    weights = [0.25, 0.5, 0.25]
    total = jnp.zeros((padded.shape[0], depth_cells, x_cells, padded.shape[3]), jnp.float32)
    for shift_z in range(3):
        for shift_x in range(3):
            total = (
                total
                + weights[shift_z]
                * weights[shift_x]
                * padded[:, shift_z : shift_z + depth_cells, shift_x : shift_x + x_cells, :]
            )
    return total


def shards(partial_grads, model, tilt, widths, step_length):
    local = partial_grads[0]
    depth_local = local.shape[1]
    x_local = model.shape[2]
    y_cells = model.shape[3]
    summed = lax.psum_scatter(
        local.astype(jnp.float32).astype(jnp.bfloat16), "shot", scatter_dimension=2, tiled=True
    )
    gradient = summed.reshape(3, depth_local, x_local * y_cells)
    pencil = exchange_by_chip(gradient, (("slab_0", "slab_1", "slab_2"), "slab_3"), (1, 0), 2, 1)
    smoothed_list = []
    for which in range(3):
        matrix = smoother(widths[which])
        smoothed_list.append(
            jnp.dot(matrix, pencil[which], preferred_element_type=jnp.float32).astype(jnp.bfloat16)
        )
    smoothed = jnp.stack(smoothed_list)
    returned = lax.all_to_all(smoothed, SLAB, split_axis=1, concat_axis=2, tiled=True)
    smoothed_slab = returned.reshape(3, depth_local, x_local, y_cells)
    updated = model - step_length[:, None, None, None] * smoothed_slab.astype(jnp.float32)
    rotated = rotate(updated[0], updated[1], updated[2], tilt)
    padded = padded_2(rotated, (("shot", 2), (SLAB, 1)), 1)
    return average(padded)


def solution(mesh):
    torus = Mesh(
        mesh.devices.reshape(mesh.shape["shot"], 4, 2, 4, 2),
        ("shot", "slab_0", "slab_1", "slab_2", "slab_3"),
    )
    placed = (
        P("shot", None, SLAB, None, None),
        P(None, SLAB, "shot", None),
        P(SLAB, "shot", None),
        P(),
        P(),
    )
    return jax.shard_map(
        shards, mesh=torus, in_specs=placed, out_specs=P(None, SLAB, "shot", None), check_vma=False
    )
```

profile of v0, /device:TPU:25, one launch (start us, length us, event | category | flops | bytes accessed | tf_op | source)
XLA Modules:
  0.0 232.0 jit_solution(17073340158344167490)
XLA Ops:
  7.3 1.2 fusion.1
  8.5 90.3 %reduce-scatter.2.cloned.1.call-done = bf16[3,16,16,256]{3,2,1,0:T(8,128)(2,1)} async-done(((bf16[3,16,128,256]{3,2,1,0:T(8,128)(2,1)}), bf16[3,16,16,256]{3,2,1,0:T(8,128)(2,1)}) %reduce-scatter.2.cloned.1.call-update) | async-done | bytes 393232 | tf_op jit(solution)/shard_map/reduce_scatter | solution.py:90
  98.8 1.5 reshape_reshape.3
  101.6 4.5 %all_to_all.19 = bf16[2,2,49152]{2,1,0:T(2,128)(2,1)S(1)} all-to-all(bf16[2,2,49152]{2,1,0:T(2,128)(2,1)S(1)} %reshape.78), channel_id=1, replica_groups=mesh['shot'=8,'slab_0'=4,'slab_1'=2,'slab_2'=4,'slab_3'=2] {'slab_3'}, dimensions={0} | all-to-all | bytes 786432 | tf_op jit(solution)/shard_map/all_to_all | solution.py:26
  106.9 1.2 reshape.80
  108.0 12.1 %all-to-all-start.1 = ((bf16[32,2,3072]{2,1,0:T(2,128)(2,1)}), bf16[32,2,3072]{2,1,0:T(2,128)(2,1)S(1)}, u32[]{:S(2)}, u32[]{:S(2)}) async-start(bf16[32,2,3072]{2,1,0:T(2,128)(2,1)} %reshape.80), calls=%async_computation.2 | async-start | bytes 786432 | tf_op jit(solution)/shard_map/all_to_all | solution.py:26
  120.2 1.2 fusion.2
  121.4 1.2 fusion
  122.6 18.8 %all-to-all-done.1 = bf16[32,2,3072]{2,1,0:T(2,128)(2,1)S(1)} async-done(((bf16[32,2,3072]{2,1,0:T(2,128)(2,1)}), bf16[32,2,3072]{2,1,0:T(2,128)(2,1)S(1)}, u32[]{:S(2)}, u32[]{:S(2)}) %all-to-all-start.1) | async-done | bytes 393248 | tf_op jit(solution)/shard_map/all_to_all | solution.py:26
  142.2 2.0 fusion.9
  144.1 2.0 fusion.11
  146.1 2.0 fusion.10
  148.8 1.5 reshape.82
  150.3 15.3 %all-to-all-start.2 = ((bf16[64,2,1536]{2,1,0:T(2,128)(2,1)}), bf16[64,2,1536]{2,1,0:T(2,128)(2,1)S(1)}, u32[]{:S(2)}, u32[]{:S(2)}) async-start(bf16[64,2,1536]{2,1,0:T(2,128)(2,1)} %reshape.82), calls=%async_computation.3 | async-start | bytes 786432 | tf_op jit(solution)/shard_map/all_to_all | solution.py:102
  165.6 1.0 fusion.37
  166.6 17.0 %all-to-all-done.2 = bf16[64,2,1536]{2,1,0:T(2,128)(2,1)S(1)} async-done(((bf16[64,2,1536]{2,1,0:T(2,128)(2,1)}), bf16[64,2,1536]{2,1,0:T(2,128)(2,1)S(1)}, u32[]{:S(2)}, u32[]{:S(2)}) %all-to-all-start.2) | async-done | bytes 393248 | tf_op jit(solution)/shard_map/all_to_all | solution.py:102
  185.5 1.3 multiply_subtract_fusion
  187.1 1.3 collective-permute-start
  188.4 1.3 collective-permute-start.1
  189.7 3.5 %collective-permute-done.1 = f32[3,16,1,256]{3,2,1,0:T(1,128)S(1)} collective-permute-done((f32[3,16,1,256]{3,2,1,0:T(1,128)S(1)}, f32[3,16,1,256]{3,2,1,0:T(1,128)S(1)}, u32[]{:S(2)}, u32[]{:S(2)}) %collective-permute-start.1) | collective-permute-done | bytes 49184 | tf_op jit(solution)/shard_map/ppermute | solution.py:44
  193.3 13.3 %collective-permute-start.2 = (f32[3,1,18,256]{3,2,1,0:T(8,128)S(1)}, f32[3,1,18,256]{3,2,1,0:T(8,128)S(1)}, u32[]{:S(2)}, u32[]{:S(2)}) collective-permute-start(f32[3,1,18,256]{3,2,1,0:T(8,128)S(1)} %get-tuple-element.10), channel_id=1, source_target_pairs={{0,1},{1,2},{2,3},{3,4},{4,5},{5,6},{6,7},{7,8},{8,9},{9,10},{10,1... | collective-permute-start | bytes 165896 | tf_op jit(solution)/shard_map/ppermute | solution.py:41
  206.7 1.9 collective-permute-start.3
  208.6 14.6 %collective-permute-done.3 = f32[3,1,18,256]{3,2,1,0:T(8,128)S(1)} collective-permute-done((f32[3,1,18,256]{3,2,1,0:T(8,128)S(1)}, f32[3,1,18,256]{3,2,1,0:T(8,128)S(1)}, u32[]{:S(2)}, u32[]{:S(2)}) %collective-permute-start.3) | collective-permute-done | bytes 55328 | tf_op jit(solution)/shard_map/ppermute | solution.py:44
  223.4 1.8 fusion.12
  (33 shorter events, 6.5 us)
Async XLA Ops:
  6.5 0.7 copy-start.1
  6.5 92.3 %reduce-scatter.2.cloned.1.call-start = ((), (), s32[]{:S(2)}) async-start(), calls=%async_computation.4 | async-start | bytes 3538944 | tf_op jit(solution)/shard_map/reduce_scatter | solution.py:90
  108.0 33.4 %all-to-all-start.1 = ((bf16[32,2,3072]{2,1,0:T(2,128)(2,1)}), bf16[32,2,3072]{2,1,0:T(2,128)(2,1)S(1)}, u32[]{:S(2)}, u32[]{:S(2)}) async-start(bf16[32,2,3072]{2,1,0:T(2,128)(2,1)} %reshape.80), calls=%async_computation.2 | async-start | bytes 786432 | tf_op jit(solution)/shard_map/all_to_all | solution.py:26
  148.1 17.6 %copy-start = (f32[16,16,256]{2,1,0:T(8,128)S(1)}, f32[16,16,256]{2,1,0:T(8,128)}, u32[]{:S(2)}) copy-start(f32[16,16,256]{2,1,0:T(8,128)} %param.7) | copy-start | bytes 786436
  150.3 33.3 %all-to-all-start.2 = ((bf16[64,2,1536]{2,1,0:T(2,128)(2,1)}), bf16[64,2,1536]{2,1,0:T(2,128)(2,1)S(1)}, u32[]{:S(2)}, u32[]{:S(2)}) async-start(bf16[64,2,1536]{2,1,0:T(2,128)(2,1)} %reshape.82), calls=%async_computation.3 | async-start | bytes 786432 | tf_op jit(solution)/shard_map/all_to_all | solution.py:102
  184.5 0.9 copy-start.2
  187.1 2.6 %collective-permute-start = (f32[3,16,1,256]{3,2,1,0:T(1,128)S(1)}, f32[3,16,1,256]{3,2,1,0:T(1,128)S(1)}, u32[]{:S(2)}, u32[]{:S(2)}) collective-permute-start(f32[3,16,1,256]{3,2,1,0:T(1,128)S(1)} %get-tuple-element.12), channel_id=1, source_target_pairs={{0,64},{64,128},{128,192},{192,256},{256,320},{320,384},{384,448},... | collective-permute-start | bytes 147464 | tf_op jit(solution)/shard_map/ppermute | solution.py:41
  188.4 4.8 %collective-permute-start.1 = (f32[3,16,1,256]{3,2,1,0:T(1,128)S(1)}, f32[3,16,1,256]{3,2,1,0:T(1,128)S(1)}, u32[]{:S(2)}, u32[]{:S(2)}) collective-permute-start(f32[3,16,1,256]{3,2,1,0:T(1,128)S(1)} %get-tuple-element.13), channel_id=1, source_target_pairs={{64,0},{128,64},{192,128},{256,192},{320,256},{384,320},{448,384},... | collective-permute-start | bytes 147464 | tf_op jit(solution)/shard_map/ppermute | solution.py:44
  193.3 15.3 %collective-permute-start.2 = (f32[3,1,18,256]{3,2,1,0:T(8,128)S(1)}, f32[3,1,18,256]{3,2,1,0:T(8,128)S(1)}, u32[]{:S(2)}, u32[]{:S(2)}) collective-permute-start(f32[3,1,18,256]{3,2,1,0:T(8,128)S(1)} %get-tuple-element.10), channel_id=1, source_target_pairs={{0,1},{1,2},{2,3},{3,4},{4,5},{5,6},{6,7},{7,8},{8,9},{9,10},{10,1... | collective-permute-start | bytes 165896 | tf_op jit(solution)/shard_map/ppermute | solution.py:41
  206.7 16.5 %collective-permute-start.3 = (f32[3,1,18,256]{3,2,1,0:T(8,128)S(1)}, f32[3,1,18,256]{3,2,1,0:T(8,128)S(1)}, u32[]{:S(2)}, u32[]{:S(2)}) collective-permute-start(f32[3,1,18,256]{3,2,1,0:T(8,128)S(1)} %get-tuple-element.11), channel_id=1, source_target_pairs={{1,0},{2,1},{3,2},{4,3},{5,4},{6,5},{7,6},{8,7},{9,8},{10,9},{11,1... | collective-permute-start | bytes 165896 | tf_op jit(solution)/shard_map/ppermute | solution.py:44
Sparse Core Ops, SparseCore 0:
  10.2 88.5 reduce-scatter.1
where the time goes:
time: 233 us; the launch traced here: 232 us
  waiting for transfers between devices  145 us (62%)
  starting transfers between devices  45.3 us (19%)
  between operations  13.7 us (6%)
  local copies, waits for them, and re-layouts  10.3 us (4%)
  other arithmetic  7.4 us (3%)
  matrix products  5.87 us (3%)
  blocking collectives  4.52 us (2%)
    reduce_scatter x1, waiting for transfers between devices, shards(): lax.psum_scatter(local.astype(jnp.float32).astype(jnp.bfloat16), 'shot',...  90.3 us
    all_to_all x1, waiting for transfers between devices, moved_by_axis(): filled = lax.all_to_all(filled, axes[k], k, k, tiled=True)  18.8 us
    ppermute x2, waiting for transfers between devices, padded_2(): lax.ppermute(lax.slice_in_dim(block, 0, width, axis=dim), axis, backward)  18.1 us
    all_to_all x1, waiting for transfers between devices, shards(): lax.all_to_all(smoothed, SLAB, split_axis=1, concat_axis=2, tiled=True)  17 us
    all_to_all x1, starting transfers between devices, shards(): lax.all_to_all(smoothed, SLAB, split_axis=1, concat_axis=2, tiled=True)  15.3 us
    ppermute x2, starting transfers between devices, padded_2(): lax.ppermute(lax.slice_in_dim(block, block.shape[dim] - width, None, axis...  14.6 us
    all_to_all x1, starting transfers between devices, moved_by_axis(): filled = lax.all_to_all(filled, axes[k], k, k, tiled=True)  12.1 us
    dot_general x3, matrix products, shards(): jnp.dot(matrix, pencil[which], preferred_element_type=jnp.float32)  5.87 us
  transfers between devices with their start and end apart: 7, of which 5 were waited for; matrix products, arithmetic and copies ran while one was open for 2% of the time, Pallas kernels for 0%

commit v1 on v0

v1 whole, which is shorter than its diff:
```python
import jax
import jax.numpy as jnp
from jax import lax
from jax.experimental import pallas as pl
from jax.experimental.pallas import tpu as pltpu
from jax.sharding import PartitionSpec as P

MESH = pl.DeviceIdType.MESH
F32 = jnp.float32
BF16 = jnp.bfloat16

SHOTS = 8
SLABS = 64
LAST = SHOTS - 1
ROWS = 16
HALF = 128
NZ = ROWS * SLABS
PIECE = 8
SPLIT = ROWS // PIECE
PER_PARAM = SHOTS * SPLIT
PIECES = 3 * PER_PARAM
SKEW = 4
LAG = 8
BLOCK = 256
BUILD = 128
STEPS_BUILD = 3 * NZ // BUILD


def kernel(
    grads, model, tilt, widths, step, out,
    held, turn, parts, pencil, matrix, product, back, flat, wave, rot, border, corner, side, near, edge,
    stream_send, stream_recv, part_send, part_recv, back_send, back_recv, halo_send, halo_recv,
):
    shot = lax.axis_index("shot")
    slab = lax.axis_index("slab")
    upper = (slab // 8) % 2
    rank_0 = shot + upper * (LAST - 2 * shot)
    sign_0 = 1 - 2 * upper
    ranks = (rank_0, LAST - rank_0)
    signs = (sign_0, -sign_0)
    is_end = (rank_0 == 0) | (rank_0 == LAST)
    end_half = jnp.where(rank_0 == LAST, 0, 1)
    slot_own = slab % 8
    pair_own = slab // 8
    chunk_own = slot_own // 2 + 4 * (slot_own % 2)

    has = {"low": shot > 0, "high": shot < LAST}
    deep = {"low": slab > 0, "high": slab < SLABS - 1}
    corner[...] = jnp.zeros_like(corner)

    @pl.when(jnp.logical_not(deep["low"]))
    def _():
        rot[:, :, 0:ROWS] = jnp.zeros((2, 3, ROWS, HALF), F32)

    @pl.when(jnp.logical_not(deep["high"]))
    def _():
        rot[:, :, ROWS * (ROWS + 1) :] = jnp.zeros((2, 3, ROWS, HALF), F32)

    def send_piece(src, h, k):
        pltpu.make_async_remote_copy(
            src_ref=src, dst_ref=held.at[h, k], send_sem=stream_send.at[h], recv_sem=stream_recv.at[h, k],
            device_id={"shot": shot + signs[h], "slab": slab}, device_id_type=MESH,
        ).start()

    def owner_of(h, g):
        high = (g // 8) % 2
        flip = high + h - 2 * high * h
        return LAST - LAST * flip

    def piece(h, k):
        rank = ranks[h]
        p = k // PER_PARAM
        rest = k % PER_PARAM
        slot = (rest // SPLIT + slot_own) % 8
        chunk = slot // 2 + 4 * (slot % 2)
        z0 = (rest % SPLIT) * PIECE
        x0 = pl.multiple_of(chunk * ROWS, ROWS)
        own = grads.at[p, pl.ds(z0, PIECE), pl.ds(x0, ROWS), pl.ds(h * HALF, HALF)]

        @pl.when(rank == 0)
        def _():
            send_piece(own, h, k)

        @pl.when(rank > 0)
        def _():
            pltpu.make_async_copy(held.at[h, k], held.at[h, k], stream_recv.at[h, k]).wait()

        @pl.when((rank > 0) & (rank < LAST))
        def _():
            held[h, k] = (held[h, k].astype(F32) + own[...].astype(F32)).astype(BF16)
            send_piece(held.at[h, k], h, k)

        @pl.when(rank == LAST)
        def _():
            total = held[h, k].astype(F32) + own[...].astype(F32)
            r0 = pl.multiple_of(z0 * ROWS, PIECE * ROWS)
            turn[pl.ds(r0, PIECE * ROWS), :] = total.reshape(PIECE * ROWS, HALF)

            @pl.when(rest % SPLIT == SPLIT - 1)
            def _():
                for j in range(8):
                    g = 8 * j + slot
                    for i in range(2):
                        parts[p, g, :, i * HALF : (i + 1) * HALF] = turn[
                            pl.ds(2 * j + i, ROWS, stride=ROWS), :
                        ].astype(BF16)

                def to_owner(j, carry):
                    g = 8 * j + slot
                    d0 = pl.multiple_of(slab * ROWS, ROWS)

                    @pl.when(g != slab)
                    def _():
                        pltpu.make_async_remote_copy(
                            src_ref=parts.at[p, g], dst_ref=pencil.at[p, pl.ds(d0, ROWS), :],
                            send_sem=part_send, recv_sem=part_recv.at[p],
                            device_id={"shot": owner_of(h, g), "slab": g}, device_id_type=MESH,
                        ).start()

                    @pl.when(g == slab)
                    def _():
                        pltpu.make_async_copy(
                            parts.at[p, g], pencil.at[p, pl.ds(d0, ROWS), :], part_recv.at[p]
                        ).start()

                    return carry

                lax.fori_loop(0, 8, to_owner, 0)

    def build(t):
        p = t // (NZ // BUILD)
        first = (t % (NZ // BUILD)) * BUILD

        def rows(r, carry):
            lane = lax.broadcasted_iota(jnp.int32, (ROWS, BUILD), 1)
            sub = lax.broadcasted_iota(jnp.int32, (ROWS, BUILD), 0)
            three = widths[:, pl.ds(pl.multiple_of(first, BUILD), BUILD)]
            width_row = jnp.where(p == 0, three[0:1], jnp.where(p == 1, three[1:2], three[2:3]))
            width = jnp.sum(jnp.where(lane == sub + r * ROWS, width_row, 0.0), axis=1, keepdims=True)
            scale = -0.5 / (width * width)
            column = lax.broadcasted_iota(jnp.int32, (ROWS, NZ), 1)
            row = lax.broadcasted_iota(jnp.int32, (ROWS, NZ), 0) + (first + r * ROWS)
            offset = (column - row).astype(F32)
            bell = jnp.exp(offset * offset * scale)
            inverse = 1.0 / jnp.sum(bell, axis=1, keepdims=True)
            r0 = pl.multiple_of(first + r * ROWS, ROWS)
            matrix[p, pl.ds(r0, ROWS), :] = (bell * inverse).astype(BF16)
            return carry

        lax.fori_loop(0, BUILD // ROWS, rows, 0)

    def smooth(p):
        pltpu.make_async_copy(pencil.at[p], pencil.at[p], part_recv.at[p]).wait()

        def block(b, carry):
            which = (b + slab // ROWS) % (NZ // BLOCK)
            r0 = pl.multiple_of(which * BLOCK, BLOCK)
            value = jnp.dot(matrix[p, pl.ds(r0, BLOCK), :], pencil[p], preferred_element_type=F32)
            d0 = which * (BLOCK // ROWS)
            product[p, pl.ds(d0, BLOCK // ROWS)] = value.astype(BF16).reshape(BLOCK // ROWS, ROWS, 2 * HALF)

            def to_slab(i, inner):
                d = d0 + (i + slab) % (BLOCK // ROWS)
                here = (d == slab) & (chunk_own == shot)

                @pl.when(jnp.logical_not(here))
                def _():
                    pltpu.make_async_remote_copy(
                        src_ref=product.at[p, d], dst_ref=back.at[end_half, pair_own, p],
                        send_sem=back_send, recv_sem=back_recv,
                        device_id={"shot": chunk_own, "slab": d}, device_id_type=MESH,
                    ).start()

                @pl.when(here)
                def _():
                    pltpu.make_async_copy(
                        product.at[p, d], back.at[end_half, pair_own, p], back_recv
                    ).start()

                return inner

            lax.fori_loop(0, BLOCK // ROWS, to_slab, 0)
            return carry

        lax.fori_loop(0, NZ // BLOCK, block, 0)

    def at_step(t, carry):
        for h in range(2):
            k = t - SKEW * ranks[h]

            @pl.when((k >= 0) & (k < PIECES))
            def _():
                piece(h, k)

        @pl.when(is_end & (t < STEPS_BUILD))
        def _():
            build(t)

        after = t - SKEW * LAST - PER_PARAM - LAG

        @pl.when(is_end & (after >= 0) & (after % PER_PARAM == 0))
        def _():
            smooth(after // PER_PARAM)

        return carry

    lax.fori_loop(0, SKEW * LAST + PIECES + LAG + 1, at_step, 0)

    def waves(z, carry):
        angle = tilt[z]
        wave[0, z] = jnp.cos(angle)
        wave[1, z] = jnp.sin(angle)
        return carry

    lax.fori_loop(0, ROWS, waves, 0)

    pltpu.make_async_copy(back, back, back_recv).wait()

    for h in range(2):
        ys = slice(h * HALF, (h + 1) * HALF)
        for p in range(3):
            for j in range(8):
                for i in range(2):
                    x = 2 * j + i
                    flat[p, x * ROWS : (x + 1) * ROWS, :] = back[h, j, p, :, i * HALF : (i + 1) * HALF].astype(F32)

        def update(z, carry):
            new = [
                model[p, z, :, ys] - step[p] * flat[p, pl.ds(z, ROWS, stride=ROWS), :]
                for p in range(3)
            ]
            squared = new[0] * new[0]
            along = squared * (1.0 + 2.0 * new[1])
            normal = squared * (1.0 + 2.0 * new[2])
            cosine = wave[0, z, :, ys]
            sine = wave[1, z, :, ys]
            cc = cosine * cosine
            ss = sine * sine
            values = (along * cc + squared * ss, along * ss + squared * cc, (normal - squared) * (sine * cosine))
            for n in range(3):
                r0 = pl.multiple_of((z + 1) * ROWS, ROWS)
                rot[h, n, pl.ds(r0, ROWS), :] = values[n]
            return carry

        lax.fori_loop(0, ROWS, update, 0)
        for n in range(3):
            border[0, n, :, ys] = rot[h, n, pl.ds(ROWS, ROWS, stride=ROWS), :]
            border[1, n, :, ys] = rot[h, n, pl.ds(2 * ROWS - 1, ROWS, stride=ROWS), :]

    for s in range(2):
        for n in range(3):
            corner[s, 0, n : n + 1, :] = border[s, n, 0:1, :]
            corner[s, 1, n : n + 1, :] = border[s, n, ROWS - 1 : ROWS, :]

    moves = []
    for index, (dx, dz) in enumerate(
        ((0, 1), (0, -1), (1, 0), (-1, 0), (1, 1), (1, -1), (-1, 1), (-1, -1))
    ):
        xs = 1 if dx > 0 else 0
        zs = 1 if dz > 0 else 0
        if dx == 0:
            source = rot.at[:, :, pl.ds(ROWS * (ROWS if dz > 0 else 1), ROWS), :]
            target = rot.at[:, :, pl.ds(0 if dz > 0 else ROWS * (ROWS + 1), ROWS), :]
        elif dz == 0:
            source = border.at[xs]
            target = side.at[1 - xs, :, pl.ds(8, ROWS), :]
        else:
            source = corner.at[xs, zs]
            target = near.at[1 - xs, 1 - zs]
        copy = pltpu.make_async_remote_copy(
            src_ref=source, dst_ref=target, send_sem=halo_send.at[index], recv_sem=halo_recv.at[index],
            device_id={"shot": shot + dx, "slab": slab + dz}, device_id_type=MESH,
        )
        goes = (shot + dx >= 0) & (shot + dx < SHOTS) & (slab + dz >= 0) & (slab + dz < SLABS)
        comes = (shot - dx >= 0) & (shot - dx < SHOTS) & (slab - dz >= 0) & (slab - dz < SLABS)
        moves.append((copy, goes, comes, target, dx, dz))

    for copy, goes, comes, target, dx, dz in moves:
        @pl.when(goes)
        def _():
            copy.start()

        if dx != 0:
            @pl.when(jnp.logical_not(comes))
            def _():
                target[...] = jnp.zeros(target.shape, F32)

    for h in range(2):
        @pl.when(ranks[h] < LAST)
        def _():
            pltpu.make_async_copy(held.at[h], held.at[h], stream_send.at[h]).wait()

    @pl.when(is_end)
    def _():
        others = parts.at[:, pl.ds(0, SLABS - 1)]
        pltpu.make_async_copy(others, others, part_send).wait()

    @pl.when(is_end & (chunk_own == shot))
    def _():
        others = product.at[:, pl.ds(0, SLABS - 1)]
        pltpu.make_async_copy(others, others, back_send).wait()

    @pl.when(is_end & (chunk_own != shot))
    def _():
        pltpu.make_async_copy(product, product, back_send).wait()

    for copy, goes, comes, target, dx, dz in moves:
        @pl.when(comes)
        def _():
            copy.wait_recv()

    for s in range(2):
        for n in range(3):
            side[s, n, 7:8, :] = near[s, 0, n : n + 1, :]
            side[s, n, 8 + ROWS : 9 + ROWS, :] = near[s, 1, n : n + 1, :]
            edge[s, n] = (
                0.25 * (side[s, n, 7 : 7 + ROWS, :] + side[s, n, 9 : 9 + ROWS, :]) + 0.5 * side[s, n, 8 : 8 + ROWS, :]
            )

    def average(group, carry):
        x_at = lax.broadcasted_iota(jnp.int32, (ROWS, HALF), 0)
        z0 = pl.multiple_of(group * 8, 8)
        for n in range(3):
            for h in range(2):
                ys = slice(h * HALF, (h + 1) * HALF)
                low = edge[0, n, pl.ds(z0, 8), ys]
                high = edge[1, n, pl.ds(z0, 8), ys]
                for i in range(8):
                    three = [
                        rot[h, n, pl.ds(pl.multiple_of((z0 + i + j) * ROWS, ROWS), ROWS), :] for j in range(3)
                    ]
                    mean = 0.25 * (three[0] + three[2]) + 0.5 * three[1]
                    before = jnp.where(x_at == 0, low[i : i + 1], pltpu.roll(mean, 1, 0))
                    after = jnp.where(x_at == ROWS - 1, high[i : i + 1], pltpu.roll(mean, ROWS - 1, 0))
                    out[n, z0 + i, :, ys] = 0.25 * (before + after) + 0.5 * mean
        return carry

    lax.fori_loop(0, ROWS // 8, average, 0)

    for copy, goes, comes, target, dx, dz in moves:
        @pl.when(goes)
        def _():
            copy.wait_send()


def shards(partial_grads, model, tilt, widths, step_length):
    vmem = pl.BlockSpec(memory_space=pltpu.VMEM)
    wide = 2 * HALF
    return pl.pallas_call(
        kernel,
        out_shape=jax.ShapeDtypeStruct(model.shape, F32),
        in_specs=[vmem, vmem, vmem, vmem, pl.BlockSpec(memory_space=pltpu.SMEM)],
        out_specs=vmem,
        scratch_shapes=[
            pltpu.VMEM((2, PIECES, PIECE, ROWS, HALF), BF16),
            pltpu.VMEM((ROWS * ROWS, HALF), F32),
            pltpu.VMEM((3, SLABS, ROWS, wide), BF16),
            pltpu.VMEM((3, NZ, wide), BF16),
            pltpu.VMEM((3, NZ, NZ), BF16),
            pltpu.VMEM((3, SLABS, ROWS, wide), BF16),
            pltpu.VMEM((2, 8, 3, ROWS, wide), BF16),
            pltpu.VMEM((3, ROWS * ROWS, HALF), F32),
            pltpu.VMEM((2, ROWS, ROWS, wide), F32),
            pltpu.VMEM((2, 3, (ROWS + 2) * ROWS, HALF), F32),
            pltpu.VMEM((2, 3, ROWS, wide), F32),
            pltpu.VMEM((2, 2, 8, wide), F32),
            pltpu.VMEM((2, 3, 2 * ROWS, wide), F32),
            pltpu.VMEM((2, 2, 8, wide), F32),
            pltpu.VMEM((2, 3, ROWS, wide), F32),
            pltpu.SemaphoreType.DMA((2,)),
            pltpu.SemaphoreType.DMA((2, PIECES)),
            pltpu.SemaphoreType.DMA,
            pltpu.SemaphoreType.DMA((3,)),
            pltpu.SemaphoreType.DMA,
            pltpu.SemaphoreType.DMA,
            pltpu.SemaphoreType.DMA((8,)),
            pltpu.SemaphoreType.DMA((8,)),
        ],
        compiler_params=pltpu.CompilerParams(has_side_effects=True, vmem_limit_bytes=48 * 1024 * 1024),
    )(partial_grads[0], model, tilt, widths, step_length)


def solution(mesh):
    placed = (
        P("shot", None, "slab", None, None),
        P(None, "slab", "shot", None),
        P("slab", "shot", None),
        P(),
        P(),
    )
    return jax.shard_map(
        shards, mesh=mesh, in_specs=placed, out_specs=P(None, "slab", "shot", None), check_vma=False
    )
```

time: 233 us -> 159 us (0.68)
  the two profiles are of different devices: /device:TPU:25 before, /device:TPU:6 now
where the time goes in v1:
time: 159 us
  Pallas kernels  153 us (96%)
  local copies, waits for them, and re-layouts  6.22 us (4%)
    pallas_call x1, Pallas kernels, shards(): pl.pallas_call(kernel, out_shape=jax.ShapeDtypeStruct(model.shape, F32),...  153 us
    unnamed x11, local copies, waits for them, and re-layouts  6.22 us

profile of v1, /device:TPU:6, one launch (start us, length us, event | category | flops | bytes accessed | tf_op | source)
XLA Modules:
  0.0 158.8 jit_solution(11085479522190897736)
XLA Ops:
  0.0 0.0 copy-start
  0.0 1.9 %copy-done = bf16[1,3,16,128,256]{4,3,2,1,0:T(8,128)(2,1)S(1)} copy-done((bf16[1,3,16,128,256]{4,3,2,1,0:T(8,128)(2,1)S(1)}, bf16[1,3,16,128,256]{4,3,2,1,0:T(8,128)(2,1)}, u32[]{:S(2)}) %copy-start) | copy-done | bytes 3145752
  1.9 0.0 copy-start.1
  1.9 1.1 copy-done.1
  3.0 0.0 copy-start.2
  3.0 0.9 copy-done.2
  4.0 0.0 copy-start.3
  4.0 0.7 copy-done.3
  4.7 0.0 copy-start.4
  4.7 0.7 copy-done.4
  5.3 152.5 %shard_map.55 = f32[3,16,16,256]{3,2,1,0:T(8,128)S(1)} custom-call(bf16[3,16,128,256]{3,2,1,0:T(8,128)(2,1)S(1)} %bitcast.1, f32[3,16,16,256]{3,2,1,0:T(8,128)S(1)} %copy-done.1, f32[16,16,256]{2,1,0:T(8,128)S(1)} %copy-done.2, f32[3,1024]{1,0:T(4,128)S(1)} %copy-done.3, f32[3]{0:T(128)S(1)} %copy-done.4), custom_call_target="tpu_custom_call" | custom-call | tf_op jit(solution)/shard_map/pallas_call | solution.py:349
  157.9 0.9 copy.7
Async XLA Ops:
  0.0 1.9 %copy-start = (bf16[1,3,16,128,256]{4,3,2,1,0:T(8,128)(2,1)S(1)}, bf16[1,3,16,128,256]{4,3,2,1,0:T(8,128)(2,1)}, u32[]{:S(2)}) copy-start(bf16[1,3,16,128,256]{4,3,2,1,0:T(8,128)(2,1)} %param.5) | copy-start | bytes 9437188
  1.9 1.1 copy-start.1
  3.0 0.9 copy-start.2
  4.0 0.7 copy-start.3
  4.7 0.7 copy-start.4

commit v2 on v1

--- a/solution.py
+++ b/solution.py
@@ -22,14 +22,15 @@
 SKEW = 4
 LAG = 8
 BLOCK = 256
+UNROLL = 4
 BUILD = 128
 STEPS_BUILD = 3 * NZ // BUILD
 
 
 def kernel(
-    grads, model, tilt, widths, step, out,
-    held, turn, parts, pencil, matrix, product, back, flat, wave, rot, border, corner, side, near, edge,
-    stream_send, stream_recv, part_send, part_recv, back_send, back_recv, halo_send, halo_recv,
+    grads_hbm, model_hbm, tilt_hbm, widths_hbm, step_hbm, out,
+    grads, model, tilt, widths, step, held, turn, parts, pencil, matrix, product, back, flat, wave, rot, border, corner, side, near, edge,
+    load, stream_send, stream_recv, part_send, part_recv, back_send, back_recv, halo_send, halo_recv,
 ):
     shot = lax.axis_index("shot")
     slab = lax.axis_index("slab")
@@ -44,6 +45,40 @@
     pair_own = slab // 8
     chunk_own = slot_own // 2 + 4 * (slot_own % 2)
 
+    def owner_of(h, g):
+        high = (g // 8) % 2
+        flip = high + h - 2 * high * h
+        return LAST - LAST * flip
+
+    loads = [
+        pltpu.make_async_copy(source, target, load.at[n])
+        for n, (source, target) in enumerate(
+            ((grads_hbm, grads), (widths_hbm, widths), (tilt_hbm, tilt), (model_hbm, model), (step_hbm, step))
+        )
+    ]
+    for copy in loads:
+        copy.start()
+    barrier = pltpu.get_barrier_semaphore()
+
+    @pl.when(shot > 0)
+    def _():
+        pl.semaphore_signal(barrier, inc=1, device_id={"shot": shot - 1, "slab": slab}, device_id_type=MESH)
+
+    @pl.when(shot < LAST)
+    def _():
+        pl.semaphore_signal(barrier, inc=1, device_id={"shot": shot + 1, "slab": slab}, device_id_type=MESH)
+
+    @pl.when(is_end)
+    def _():
+        def greet(i, carry):
+            g = (slab + i) % SLABS
+            pl.semaphore_signal(
+                barrier, inc=1, device_id={"shot": owner_of(end_half, g), "slab": g}, device_id_type=MESH
+            )
+            return carry
+
+        lax.fori_loop(1, SLABS, greet, 0)
+
     has = {"low": shot > 0, "high": shot < LAST}
     deep = {"low": slab > 0, "high": slab < SLABS - 1}
     corner[...] = jnp.zeros_like(corner)
@@ -61,11 +96,6 @@
             src_ref=src, dst_ref=held.at[h, k], send_sem=stream_send.at[h], recv_sem=stream_recv.at[h, k],
             device_id={"shot": shot + signs[h], "slab": slab}, device_id_type=MESH,
         ).start()
-
-    def owner_of(h, g):
-        high = (g // 8) % 2
-        flip = high + h - 2 * high * h
-        return LAST - LAST * flip
 
     def piece(h, k):
         rank = ranks[h]
@@ -75,11 +105,12 @@
         chunk = slot // 2 + 4 * (slot % 2)
         z0 = (rest % SPLIT) * PIECE
         x0 = pl.multiple_of(chunk * ROWS, ROWS)
-        own = grads.at[p, pl.ds(z0, PIECE), pl.ds(x0, ROWS), pl.ds(h * HALF, HALF)]
+        where = (p, pl.ds(z0, PIECE), pl.ds(x0, ROWS), pl.ds(h * HALF, HALF))
+        own = grads.at[where]
 
         @pl.when(rank == 0)
         def _():
-            send_piece(own, h, k)
+            send_piece(grads_hbm.at[where], h, k)
 
         @pl.when(rank > 0)
         def _():
@@ -147,7 +178,7 @@
             matrix[p, pl.ds(r0, ROWS), :] = (bell * inverse).astype(BF16)
             return carry
 
-        lax.fori_loop(0, BUILD // ROWS, rows, 0)
+        lax.fori_loop(0, BUILD // ROWS, rows, 0, unroll=UNROLL)
 
     def smooth(p):
         pltpu.make_async_copy(pencil.at[p], pencil.at[p], part_recv.at[p]).wait()
@@ -184,6 +215,10 @@
 
         lax.fori_loop(0, NZ // BLOCK, block, 0)
 
+    pl.semaphore_wait(barrier, jnp.where(is_end, SLABS, 2))
+    loads[0].wait()
+    loads[1].wait()
+
     def at_step(t, carry):
         for h in range(2):
             k = t - SKEW * ranks[h]
@@ -205,6 +240,9 @@
         return carry
 
     lax.fori_loop(0, SKEW * LAST + PIECES + LAG + 1, at_step, 0)
+
+    for copy in loads[2:]:
+        copy.wait()
 
     def waves(z, carry):
         angle = tilt[z]
@@ -345,13 +383,19 @@
 
 def shards(partial_grads, model, tilt, widths, step_length):
     vmem = pl.BlockSpec(memory_space=pltpu.VMEM)
+    hbm = pl.BlockSpec(memory_space=pl.ANY)
     wide = 2 * HALF
     return pl.pallas_call(
         kernel,
         out_shape=jax.ShapeDtypeStruct(model.shape, F32),
-        in_specs=[vmem, vmem, vmem, vmem, pl.BlockSpec(memory_space=pltpu.SMEM)],
+        in_specs=[hbm] * 5,
         out_specs=vmem,
         scratch_shapes=[
+            pltpu.VMEM(partial_grads.shape[1:], BF16),
+            pltpu.VMEM(model.shape, F32),
+            pltpu.VMEM(tilt.shape, F32),
+            pltpu.VMEM(widths.shape, F32),
+            pltpu.SMEM(step_length.shape, F32),
             pltpu.VMEM((2, PIECES, PIECE, ROWS, HALF), BF16),
             pltpu.VMEM((ROWS * ROWS, HALF), F32),
             pltpu.VMEM((3, SLABS, ROWS, wide), BF16),
@@ -367,6 +411,7 @@
             pltpu.VMEM((2, 3, 2 * ROWS, wide), F32),
             pltpu.VMEM((2, 2, 8, wide), F32),
             pltpu.VMEM((2, 3, ROWS, wide), F32),
+            pltpu.SemaphoreType.DMA((5,)),
             pltpu.SemaphoreType.DMA((2,)),
             pltpu.SemaphoreType.DMA((2, PIECES)),
             pltpu.SemaphoreType.DMA,
@@ -376,7 +421,9 @@
             pltpu.SemaphoreType.DMA((8,)),
             pltpu.SemaphoreType.DMA((8,)),
         ],
-        compiler_params=pltpu.CompilerParams(has_side_effects=True, vmem_limit_bytes=48 * 1024 * 1024),
+        compiler_params=pltpu.CompilerParams(
+            collective_id=0, has_side_effects=True, vmem_limit_bytes=60 * 1024 * 1024
+        ),
     )(partial_grads[0], model, tilt, widths, step_length)
 
 

time: 159 us -> 123 us (0.77); the launches traced: 159 us -> 121 us
  Pallas kernels: 153 us -> 119 us
  local copies, waits for them, and re-layouts: 6.22 us -> 2.06 us
    pallas_call x1, Pallas kernels: 153 us -> 119 us  [shards(): pl.pallas_call(kernel, out_shape=jax.ShapeDtypeStruct(model.shape, F32),...]
    unnamed x11 -> x1, local copies, waits for them, and re-layouts: 6.22 us -> 2.06 us
where the time goes in v2:
time: 123 us; the launch traced here: 121 us
  Pallas kernels  119 us (97%)
  local copies, waits for them, and re-layouts  2.06 us (2%)
    pallas_call x1, Pallas kernels, shards(): pl.pallas_call(kernel, out_shape=jax.ShapeDtypeStruct(model.shape, F32),...  119 us

profile of v2, /device:TPU:6, one launch (start us, length us, event | category | flops | bytes accessed | tf_op | source)
XLA Modules:
  0.0 121.1 jit_solution(16174027378654478096)
XLA Ops:
  0.0 119.0 %shard_map.55 = f32[3,16,16,256]{3,2,1,0:T(8,128)} custom-call(bf16[3,16,128,256]{3,2,1,0:T(8,128)(2,1)} %bitcast.1, f32[3,16,16,256]{3,2,1,0:T(8,128)} %model_hbm.1, f32[16,16,256]{2,1,0:T(8,128)} %tilt_hbm.1, f32[3,1024]{1,0:T(4,128)} %widths_hbm.1, f32[3]{0:T(128)} %step_hbm.1), custom_call_target="tpu_custom_call" | custom-call | tf_op jit(solution)/shard_map/pallas_call | solution.py:388
  119.0 2.1 %copy.7 = f32[3,16,16,256]{3,2,1,0:T(8,128)} copy(f32[3,16,16,256]{3,2,1,0:T(8,128)} %shard_map.55) | data formatting | bytes 1572864

commit v3 on v2

--- a/solution.py
+++ b/solution.py
@@ -19,18 +19,28 @@
 SPLIT = ROWS // PIECE
 PER_PARAM = SHOTS * SPLIT
 PIECES = 3 * PER_PARAM
-SKEW = 4
-LAG = 8
+SKEW = 11
+LAG = 16
 BLOCK = 256
 UNROLL = 4
+FILL = (SKEW * LAST) // 2
+GREET_STEPS = (SLABS - 1) // 3
 BUILD = 128
 STEPS_BUILD = 3 * NZ // BUILD
+
+
+def chunk_of(slot):
+    return slot // 2 + (slot % 2) * (LAST - 2 * (slot // 2))
+
+
+def owner_slab(pair, slot):
+    return (pair % 4) * 16 + (pair // 4) * 8 + ((pair + slot) % 4) * 2 + slot // 4
 
 
 def kernel(
     grads_hbm, model_hbm, tilt_hbm, widths_hbm, step_hbm, out,
     grads, model, tilt, widths, step, held, turn, parts, pencil, matrix, product, back, flat, wave, rot, border, corner, side, near, edge,
-    load, stream_send, stream_recv, part_send, part_recv, back_send, back_recv, halo_send, halo_recv,
+    there, load, stream_send, stream_recv, part_send, part_recv, back_send, back_recv, halo_send, halo_recv,
 ):
     shot = lax.axis_index("shot")
     slab = lax.axis_index("slab")
@@ -41,9 +51,10 @@
     signs = (sign_0, -sign_0)
     is_end = (rank_0 == 0) | (rank_0 == LAST)
     end_half = jnp.where(rank_0 == LAST, 0, 1)
-    slot_own = slab % 8
-    pair_own = slab // 8
-    chunk_own = slot_own // 2 + 4 * (slot_own % 2)
+    slab_x, slab_y = slab // 16, (slab // 2) % 4
+    slot_own = (slab_y + 4 - slab_x) % 4 + 4 * (slab % 2)
+    pair_own = slab_x + 4 * upper
+    chunk_own = chunk_of(slot_own)
 
     def owner_of(h, g):
         high = (g // 8) % 2
@@ -56,28 +67,22 @@
             ((grads_hbm, grads), (widths_hbm, widths), (tilt_hbm, tilt), (model_hbm, model), (step_hbm, step))
         )
     ]
+    barrier = pltpu.get_barrier_semaphore()
+
+    for to in (-1, 1):
+        @pl.when((shot + to >= 0) & (shot + to < SHOTS) & (rank_0 + sign_0 * to > 0) & (rank_0 + sign_0 * to < LAST))
+        def _():
+            pl.semaphore_signal(barrier, inc=1, device_id={"shot": shot + to, "slab": slab}, device_id_type=MESH)
+
+    def greet(i, carry):
+        g = (slab + i) % SLABS
+        pl.semaphore_signal(
+            barrier, inc=1, device_id={"shot": owner_of(end_half, g), "slab": g}, device_id_type=MESH
+        )
+        return carry
+
     for copy in loads:
         copy.start()
-    barrier = pltpu.get_barrier_semaphore()
-
-    @pl.when(shot > 0)
-    def _():
-        pl.semaphore_signal(barrier, inc=1, device_id={"shot": shot - 1, "slab": slab}, device_id_type=MESH)
-
-    @pl.when(shot < LAST)
-    def _():
-        pl.semaphore_signal(barrier, inc=1, device_id={"shot": shot + 1, "slab": slab}, device_id_type=MESH)
-
-    @pl.when(is_end)
-    def _():
-        def greet(i, carry):
-            g = (slab + i) % SLABS
-            pl.semaphore_signal(
-                barrier, inc=1, device_id={"shot": owner_of(end_half, g), "slab": g}, device_id_type=MESH
-            )
-            return carry
-
-        lax.fori_loop(1, SLABS, greet, 0)
 
     has = {"low": shot > 0, "high": shot < LAST}
     deep = {"low": slab > 0, "high": slab < SLABS - 1}
@@ -97,26 +102,23 @@
             device_id={"shot": shot + signs[h], "slab": slab}, device_id_type=MESH,
         ).start()
 
-    def piece(h, k):
+    def piece(h, k, starts):
         rank = ranks[h]
         p = k // PER_PARAM
         rest = k % PER_PARAM
-        slot = (rest // SPLIT + slot_own) % 8
-        chunk = slot // 2 + 4 * (slot % 2)
+        slot = rest // SPLIT
+        chunk = chunk_of(slot)
         z0 = (rest % SPLIT) * PIECE
         x0 = pl.multiple_of(chunk * ROWS, ROWS)
         where = (p, pl.ds(z0, PIECE), pl.ds(x0, ROWS), pl.ds(h * HALF, HALF))
         own = grads.at[where]
 
-        @pl.when(rank == 0)
-        def _():
+        if starts:
             send_piece(grads_hbm.at[where], h, k)
-
-        @pl.when(rank > 0)
-        def _():
-            pltpu.make_async_copy(held.at[h, k], held.at[h, k], stream_recv.at[h, k]).wait()
-
-        @pl.when((rank > 0) & (rank < LAST))
+            return
+        pltpu.make_async_copy(held.at[h, k], held.at[h, k], stream_recv.at[h, k]).wait()
+
+        @pl.when(rank < LAST)
         def _():
             held[h, k] = (held[h, k].astype(F32) + own[...].astype(F32)).astype(BF16)
             send_piece(held.at[h, k], h, k)
@@ -130,14 +132,14 @@
             @pl.when(rest % SPLIT == SPLIT - 1)
             def _():
                 for j in range(8):
-                    g = 8 * j + slot
+                    g = owner_slab(j, slot)
                     for i in range(2):
                         parts[p, g, :, i * HALF : (i + 1) * HALF] = turn[
                             pl.ds(2 * j + i, ROWS, stride=ROWS), :
                         ].astype(BF16)
 
-                def to_owner(j, carry):
-                    g = 8 * j + slot
+                def to_owner(i, carry):
+                    g = owner_slab((i + slab) % 8, slot)
                     d0 = pl.multiple_of(slab * ROWS, ROWS)
 
                     @pl.when(g != slab)
@@ -215,31 +217,60 @@
 
         lax.fori_loop(0, NZ // BLOCK, block, 0)
 
-    pl.semaphore_wait(barrier, jnp.where(is_end, SLABS, 2))
-    loads[0].wait()
-    loads[1].wait()
+    @pl.when(jnp.logical_not(is_end))
+    def _():
+        pl.semaphore_wait(barrier, 2)
+
+    for to in (-1, 1):
+        @pl.when((shot + to >= 0) & (shot + to < SHOTS) & ((rank_0 + sign_0 * to == 0) | (rank_0 + sign_0 * to == LAST)))
+        def _():
+            pl.semaphore_signal(there, inc=1, device_id={"shot": shot + to, "slab": slab}, device_id_type=MESH)
+
+    @pl.when(is_end)
+    def _():
+        pl.semaphore_wait(there, 1)
 
     def at_step(t, carry):
         for h in range(2):
-            k = t - SKEW * ranks[h]
-
-            @pl.when((k >= 0) & (k < PIECES))
+            rank = ranks[h]
+            k = t - (SKEW * rank) // 2
+
+            @pl.when((rank == 0) & (t < PIECES // 2))
             def _():
-                piece(h, k)
+                piece(h, 2 * t, True)
+                piece(h, 2 * t + 1, True)
+
+            if h == 0:
+                @pl.when(t == 0)
+                def _():
+                    loads[0].wait()
+                    loads[1].wait()
+
+            @pl.when((rank > 0) & (k >= 0) & (k < PIECES))
+            def _():
+                piece(h, k, False)
+
+        @pl.when(is_end & (t < GREET_STEPS))
+        def _():
+            lax.fori_loop(1 + 3 * t, 4 + 3 * t, greet, 0)
 
         @pl.when(is_end & (t < STEPS_BUILD))
         def _():
             build(t)
 
-        after = t - SKEW * LAST - PER_PARAM - LAG
-
-        @pl.when(is_end & (after >= 0) & (after % PER_PARAM == 0))
+        @pl.when(is_end & (t == FILL - 1))
+        def _():
+            pl.semaphore_wait(barrier, SLABS - 1)
+
+        after = t - FILL - SPLIT * (slot_own + 1) - LAG
+
+        @pl.when(is_end & (after >= 0) & (after % PER_PARAM == 0) & (after < PIECES))
         def _():
             smooth(after // PER_PARAM)
 
         return carry
 
-    lax.fori_loop(0, SKEW * LAST + PIECES + LAG + 1, at_step, 0)
+    lax.fori_loop(0, FILL + PIECES + LAG + 1, at_step, 0)
 
     for copy in loads[2:]:
         copy.wait()
@@ -411,6 +442,7 @@
             pltpu.VMEM((2, 3, 2 * ROWS, wide), F32),
             pltpu.VMEM((2, 2, 8, wide), F32),
             pltpu.VMEM((2, 3, ROWS, wide), F32),
+            pltpu.SemaphoreType.REGULAR,
             pltpu.SemaphoreType.DMA((5,)),
             pltpu.SemaphoreType.DMA((2,)),
             pltpu.SemaphoreType.DMA((2, PIECES)),

time: 123 us -> 110 us (0.89); the launches traced: 121 us -> 110 us
  Pallas kernels: 119 us -> 108 us
    pallas_call x1, Pallas kernels: 119 us -> 108 us  [shards(): pl.pallas_call(kernel, out_shape=jax.ShapeDtypeStruct(model.shape, F32),...]
where the time goes in v3:
time: 110 us
  Pallas kernels  108 us (98%)
  local copies, waits for them, and re-layouts  2.06 us (2%)
    pallas_call x1, Pallas kernels, shards(): pl.pallas_call(kernel, out_shape=jax.ShapeDtypeStruct(model.shape, F32),...  108 us

profile of v3, /device:TPU:6, one launch (start us, length us, event | category | flops | bytes accessed | tf_op | source)
XLA Modules:
  0.0 110.1 jit_solution(9541001885972768118)
XLA Ops:
  0.0 108.1 %shard_map.55 = f32[3,16,16,256]{3,2,1,0:T(8,128)} custom-call(bf16[3,16,128,256]{3,2,1,0:T(8,128)(2,1)} %bitcast.1, f32[3,16,16,256]{3,2,1,0:T(8,128)} %model_hbm.1, f32[16,16,256]{2,1,0:T(8,128)} %tilt_hbm.1, f32[3,1024]{1,0:T(4,128)} %widths_hbm.1, f32[3]{0:T(128)} %step_hbm.1), custom_call_target="tpu_custom_call" | custom-call | tf_op jit(solution)/shard_map/pallas_call | solution.py:419
  108.1 2.1 %copy.7 = f32[3,16,16,256]{3,2,1,0:T(8,128)} copy(f32[3,16,16,256]{3,2,1,0:T(8,128)} %shard_map.55) | data formatting | bytes 1572864

commit v4 on v2

v4 whole, which is shorter than its diff:
```python
import jax
import jax.numpy as jnp
from jax import lax
from jax.experimental import pallas as pl
from jax.experimental.pallas import tpu as pltpu
from jax.sharding import PartitionSpec as P

MESH = pl.DeviceIdType.MESH
F32 = jnp.float32
BF16 = jnp.bfloat16

SHOTS = 8
SLABS = 64
LAST = SHOTS - 1
ROWS = 16
HALF = 128
QUAD = 4
QUADS = ROWS // QUAD
NZ = ROWS * SLABS
PER_PARAM = 2 * SHOTS
PIECES = 3 * PER_PARAM
BLOCK = 256
BUILD = 128
UNROLL = 4


def chunk_of(slot):
    return slot // 2 + (slot % 2) * (LAST - 2 * (slot // 2))


def kernel(
    grads_hbm, model_hbm, tilt_hbm, widths_hbm, step_hbm, out,
    mine, model, tilt, widths, step, held,
    turn, parts, pencil, matrix, product, back, flat, wave, rot, border, corner, side, near, edge,
    there, load, swap_send, swap_recv, stream_send, stream_recv, part_send, part_recv, back_send, back_recv,
    halo_send, halo_recv,
):
    shot = lax.axis_index("shot")
    slab = lax.axis_index("slab")
    core = slab % 2
    upper = (slab // 8) % 2
    slab_x, slab_y = slab // 16, (slab // 2) % 4
    other = slab + 1 - 2 * core
    turned = upper + core - 2 * upper * core
    rank = shot + turned * (LAST - 2 * shot)
    sign = 1 - 2 * turned
    is_first = rank == 0
    is_last = rank == LAST
    is_middle = (rank > 0) & (rank < LAST)
    y0 = pl.multiple_of(core * HALF, HALF)
    y0_other = pl.multiple_of((1 - core) * HALF, HALF)

    slot_own = (slab_y + 4 - slab_x) % 4 + 4 * ((upper + slab_x) % 2)
    chunk_own = chunk_of(slot_own)
    half_own = 1 - core

    def plane_of(h, high):
        flip = high + h - 2 * high * h
        return LAST - LAST * flip

    barrier = pltpu.get_barrier_semaphore()

    @pl.when(rank > 0)
    def _():
        pl.semaphore_signal(barrier, inc=1, device_id={"shot": shot - sign, "slab": slab}, device_id_type=MESH)
        pl.semaphore_signal(barrier, inc=1, device_id={"shot": shot, "slab": other}, device_id_type=MESH)

    loads = [
        pltpu.make_async_copy(source, target, load.at[n])
        for n, (source, target) in enumerate(
            (
                (grads_hbm.at[:, :, :, pl.ds(y0, HALF)], mine.at[0]),
                (widths_hbm, widths),
                (tilt_hbm, tilt),
                (model_hbm, model),
                (step_hbm, step),
            )
        )
    ]
    for copy in loads:
        copy.start()

    @pl.when(is_last)
    def _():
        pl.semaphore_wait(there, 1)

    @pl.when(jnp.logical_not(is_last))
    def _():
        pl.semaphore_wait(barrier, 2)

    @pl.when(is_first)
    def _():
        pl.semaphore_signal(there, inc=1, device_id={"shot": shot, "slab": other}, device_id_type=MESH)

    swaps = [
        pltpu.make_async_remote_copy(
            src_ref=grads_hbm.at[p, :, :, pl.ds(y0_other, HALF)], dst_ref=mine.at[1, p],
            send_sem=swap_send.at[p], recv_sem=swap_recv.at[p],
            device_id={"shot": shot, "slab": other}, device_id_type=MESH,
        )
        for p in range(3)
    ]
    for copy in swaps:
        copy.start()

    def place(k):
        p = k // PER_PARAM
        rest = k % PER_PARAM
        b = jnp.where(p == 0, rest // SHOTS, rest % 2)
        slot = jnp.where(p == 0, rest % SHOTS, rest // 2)
        return p, b, slot

    def columns(slot):
        return pl.ds(pl.multiple_of(chunk_of(slot) * ROWS, ROWS), ROWS)

    def send_piece(src, k):
        pltpu.make_async_remote_copy(
            src_ref=src, dst_ref=held.at[k], send_sem=stream_send, recv_sem=stream_recv.at[k],
            device_id={"shot": shot + sign, "slab": slab}, device_id_type=MESH,
        ).start()

    def arrived(k):
        pltpu.make_async_copy(held.at[k], held.at[k], stream_recv.at[k]).wait()

    has = {"low": shot > 0, "high": shot < LAST}
    deep = {"low": slab > 0, "high": slab < SLABS - 1}
    corner[...] = jnp.zeros_like(corner)

    @pl.when(jnp.logical_not(deep["low"]))
    def _():
        rot[:, :, 0:ROWS] = jnp.zeros((2, 3, ROWS, HALF), F32)

    @pl.when(jnp.logical_not(deep["high"]))
    def _():
        rot[:, :, ROWS * (ROWS + 1) :] = jnp.zeros((2, 3, ROWS, HALF), F32)

    def build(t):
        p = t // (NZ // BUILD)
        first = (t % (NZ // BUILD)) * BUILD

        def rows(r, carry):
            lane = lax.broadcasted_iota(jnp.int32, (ROWS, BUILD), 1)
            sub = lax.broadcasted_iota(jnp.int32, (ROWS, BUILD), 0)
            three = widths[:, pl.ds(pl.multiple_of(first, BUILD), BUILD)]
            width_row = jnp.where(p == 0, three[0:1], jnp.where(p == 1, three[1:2], three[2:3]))
            width = jnp.sum(jnp.where(lane == sub + r * ROWS, width_row, 0.0), axis=1, keepdims=True)
            scale = -0.5 / (width * width)
            column = lax.broadcasted_iota(jnp.int32, (ROWS, NZ), 1)
            row = lax.broadcasted_iota(jnp.int32, (ROWS, NZ), 0) + (first + r * ROWS)
            offset = (column - row).astype(F32)
            bell = jnp.exp(offset * offset * scale)
            inverse = 1.0 / jnp.sum(bell, axis=1, keepdims=True)
            r0 = pl.multiple_of(first + r * ROWS, ROWS)
            matrix[p, pl.ds(r0, ROWS), :] = (bell * inverse).astype(BF16)
            return carry

        lax.fori_loop(0, BUILD // ROWS, rows, 0, unroll=UNROLL)

    @pl.when(is_first)
    def _():
        def own_first(k, carry):
            send_piece(grads_hbm.at[0, :, columns(k), pl.ds(y0, HALF)], k)
            return carry

        lax.fori_loop(0, SHOTS, own_first, 0)
        loads[0].wait()
        swaps[0].wait_recv()

        def rest_of_0(k, carry):
            send_piece(mine.at[1, 0, :, columns(k - SHOTS), :], k)
            return carry

        lax.fori_loop(SHOTS, PER_PARAM, rest_of_0, 0)
        for q in range(1, 3):
            swaps[q].wait_recv()

            def both(k, carry):
                p, b, slot = place(k)
                send_piece(mine.at[b, p, :, columns(slot), :], k)
                return carry

            lax.fori_loop(q * PER_PARAM, (q + 1) * PER_PARAM, both, 0)

        def greet(i, carry):
            line = (slab // 2 + i) % (SLABS // 2)
            pl.semaphore_signal(
                barrier, inc=1,
                device_id={"shot": plane_of(half_own, (line // 4) % 2), "slab": 2 * line + half_own},
                device_id_type=MESH,
            )
            return carry

        lax.fori_loop(0, SLABS // 2, greet, 0)
        loads[1].wait()

        def build_step(t, carry):
            build(t)
            return carry

        lax.fori_loop(0, 3 * NZ // BUILD, build_step, 0)

        def smooth(p, carry):
            pltpu.make_async_copy(pencil.at[p], pencil.at[p], part_recv.at[p]).wait()

            def block(b, inner):
                which = (b + slab_x) % (NZ // BLOCK)
                r0 = pl.multiple_of(which * BLOCK, BLOCK)
                value = jnp.dot(matrix[p, pl.ds(r0, BLOCK), :], pencil[p], preferred_element_type=F32)
                d0 = which * (BLOCK // ROWS)
                product[p, pl.ds(d0, BLOCK // ROWS)] = value.astype(BF16).reshape(BLOCK // ROWS, ROWS, QUAD * HALF)

                def to_slab(i, last):
                    d = d0 + (i + slab) % (BLOCK // ROWS)
                    here = (d == slab) & (chunk_own == shot)

                    @pl.when(jnp.logical_not(here))
                    def _():
                        pltpu.make_async_remote_copy(
                            src_ref=product.at[p, d], dst_ref=back.at[half_own, slab_x, p],
                            send_sem=back_send, recv_sem=back_recv,
                            device_id={"shot": chunk_own, "slab": d}, device_id_type=MESH,
                        ).start()

                    @pl.when(here)
                    def _():
                        pltpu.make_async_copy(product.at[p, d], back.at[half_own, slab_x, p], back_recv).start()

                    return last

                lax.fori_loop(0, BLOCK // ROWS, to_slab, 0)
                return inner

            lax.fori_loop(0, NZ // BLOCK, block, 0)
            return carry

        lax.fori_loop(0, 3, smooth, 0)

    @pl.when(jnp.logical_not(is_first))
    def _():
        loads[0].wait()
        loads[1].wait()
        for copy in swaps:
            copy.wait_recv()

    @pl.when(is_middle)
    def _():
        def pass_on(k, carry):
            p, b, slot = place(k)
            arrived(k)
            held[k] = (held[k].astype(F32) + mine[b, p, :, columns(slot), :].astype(F32)).astype(BF16)
            send_piece(held.at[k], k)
            return carry

        lax.fori_loop(0, PIECES, pass_on, 0)

    @pl.when(is_last)
    def _():
        pl.semaphore_wait(barrier, SLABS // 2)

        def finish(k, carry):
            p, b, slot = place(k)
            arrived(k)
            total = held[k].astype(F32) + mine[b, p, :, columns(slot), :].astype(F32)
            turn[...] = total.reshape(ROWS * ROWS, HALF)
            d0 = pl.multiple_of(jnp.where(b == 0, slab, other) * ROWS, ROWS)
            for m in range(QUADS):
                for i in range(QUAD):
                    parts[p, b, slot, m, :, i * HALF : (i + 1) * HALF] = turn[
                        pl.ds(QUAD * m + i, ROWS, stride=ROWS), :
                    ].astype(BF16)
                high = (slot // 4 + m) % 2
                pltpu.make_async_remote_copy(
                    src_ref=parts.at[p, b, slot, m], dst_ref=pencil.at[p, pl.ds(d0, ROWS), :],
                    send_sem=part_send, recv_sem=part_recv.at[p],
                    device_id={
                        "shot": plane_of(core, high),
                        "slab": m * 16 + high * 8 + ((m + slot) % 4) * 2 + 1 - core,
                    },
                    device_id_type=MESH,
                ).start()
            return carry

        lax.fori_loop(0, PIECES, finish, 0)

    for copy in loads[2:]:
        copy.wait()

    def waves(z, carry):
        angle = tilt[z]
        wave[0, z] = jnp.cos(angle)
        wave[1, z] = jnp.sin(angle)
        return carry

    lax.fori_loop(0, ROWS, waves, 0)

    pltpu.make_async_copy(back, back, back_recv).wait()

    for h in range(2):
        ys = slice(h * HALF, (h + 1) * HALF)
        for p in range(3):
            for x in range(ROWS):
                m, i = x // QUAD, x % QUAD
                flat[p, x * ROWS : (x + 1) * ROWS, :] = back[h, m, p, :, i * HALF : (i + 1) * HALF].astype(F32)

        def update(z, carry):
            new = [
                model[p, z, :, ys] - step[p] * flat[p, pl.ds(z, ROWS, stride=ROWS), :]
                for p in range(3)
            ]
            squared = new[0] * new[0]
            along = squared * (1.0 + 2.0 * new[1])
            normal = squared * (1.0 + 2.0 * new[2])
            cosine = wave[0, z, :, ys]
            sine = wave[1, z, :, ys]
            cc = cosine * cosine
            ss = sine * sine
            values = (along * cc + squared * ss, along * ss + squared * cc, (normal - squared) * (sine * cosine))
            for n in range(3):
                r0 = pl.multiple_of((z + 1) * ROWS, ROWS)
                rot[h, n, pl.ds(r0, ROWS), :] = values[n]
            return carry

        lax.fori_loop(0, ROWS, update, 0)
        for n in range(3):
            border[0, n, :, ys] = rot[h, n, pl.ds(ROWS, ROWS, stride=ROWS), :]
            border[1, n, :, ys] = rot[h, n, pl.ds(2 * ROWS - 1, ROWS, stride=ROWS), :]

    for s in range(2):
        for n in range(3):
            corner[s, 0, n : n + 1, :] = border[s, n, 0:1, :]
            corner[s, 1, n : n + 1, :] = border[s, n, ROWS - 1 : ROWS, :]

    moves = []
    for index, (dx, dz) in enumerate(
        ((0, 1), (0, -1), (1, 0), (-1, 0), (1, 1), (1, -1), (-1, 1), (-1, -1))
    ):
        xs = 1 if dx > 0 else 0
        zs = 1 if dz > 0 else 0
        if dx == 0:
            source = rot.at[:, :, pl.ds(ROWS * (ROWS if dz > 0 else 1), ROWS), :]
            target = rot.at[:, :, pl.ds(0 if dz > 0 else ROWS * (ROWS + 1), ROWS), :]
        elif dz == 0:
            source = border.at[xs]
            target = side.at[1 - xs, :, pl.ds(8, ROWS), :]
        else:
            source = corner.at[xs, zs]
            target = near.at[1 - xs, 1 - zs]
        copy = pltpu.make_async_remote_copy(
            src_ref=source, dst_ref=target, send_sem=halo_send.at[index], recv_sem=halo_recv.at[index],
            device_id={"shot": shot + dx, "slab": slab + dz}, device_id_type=MESH,
        )
        goes = (shot + dx >= 0) & (shot + dx < SHOTS) & (slab + dz >= 0) & (slab + dz < SLABS)
        comes = (shot - dx >= 0) & (shot - dx < SHOTS) & (slab - dz >= 0) & (slab - dz < SLABS)
        moves.append((copy, goes, comes, target, dx, dz))

    for copy, goes, comes, target, dx, dz in moves:
        @pl.when(goes)
        def _():
            copy.start()

        if dx != 0:
            @pl.when(jnp.logical_not(comes))
            def _():
                target[...] = jnp.zeros(target.shape, F32)

    for copy in swaps:
        copy.wait_send()

    @pl.when(jnp.logical_not(is_last))
    def _():
        pltpu.make_async_copy(held, held, stream_send).wait()

    @pl.when(is_last)
    def _():
        pltpu.make_async_copy(parts, parts, part_send).wait()

    @pl.when(is_first & (chunk_own == shot))
    def _():
        others = product.at[:, pl.ds(0, SLABS - 1)]
        pltpu.make_async_copy(others, others, back_send).wait()

    @pl.when(is_first & (chunk_own != shot))
    def _():
        pltpu.make_async_copy(product, product, back_send).wait()

    for copy, goes, comes, target, dx, dz in moves:
        @pl.when(comes)
        def _():
            copy.wait_recv()

    for s in range(2):
        for n in range(3):
            side[s, n, 7:8, :] = near[s, 0, n : n + 1, :]
            side[s, n, 8 + ROWS : 9 + ROWS, :] = near[s, 1, n : n + 1, :]
            edge[s, n] = (
                0.25 * (side[s, n, 7 : 7 + ROWS, :] + side[s, n, 9 : 9 + ROWS, :]) + 0.5 * side[s, n, 8 : 8 + ROWS, :]
            )

    def average(group, carry):
        x_at = lax.broadcasted_iota(jnp.int32, (ROWS, HALF), 0)
        z0 = pl.multiple_of(group * 8, 8)
        for n in range(3):
            for h in range(2):
                ys = slice(h * HALF, (h + 1) * HALF)
                low = edge[0, n, pl.ds(z0, 8), ys]
                high = edge[1, n, pl.ds(z0, 8), ys]
                for i in range(8):
                    three = [
                        rot[h, n, pl.ds(pl.multiple_of((z0 + i + j) * ROWS, ROWS), ROWS), :] for j in range(3)
                    ]
                    mean = 0.25 * (three[0] + three[2]) + 0.5 * three[1]
                    before = jnp.where(x_at == 0, low[i : i + 1], pltpu.roll(mean, 1, 0))
                    after = jnp.where(x_at == ROWS - 1, high[i : i + 1], pltpu.roll(mean, ROWS - 1, 0))
                    out[n, z0 + i, :, ys] = 0.25 * (before + after) + 0.5 * mean
        return carry

    lax.fori_loop(0, ROWS // 8, average, 0)

    for copy, goes, comes, target, dx, dz in moves:
        @pl.when(goes)
        def _():
            copy.wait_send()


def shards(partial_grads, model, tilt, widths, step_length):
    vmem = pl.BlockSpec(memory_space=pltpu.VMEM)
    hbm = pl.BlockSpec(memory_space=pl.ANY)
    wide = 2 * HALF
    return pl.pallas_call(
        kernel,
        out_shape=jax.ShapeDtypeStruct(model.shape, F32),
        in_specs=[hbm] * 5,
        out_specs=vmem,
        scratch_shapes=[
            pltpu.VMEM((2, 3, ROWS, SHOTS * ROWS, HALF), BF16),
            pltpu.VMEM(model.shape, F32),
            pltpu.VMEM(tilt.shape, F32),
            pltpu.VMEM(widths.shape, F32),
            pltpu.SMEM(step_length.shape, F32),
            pltpu.VMEM((PIECES, ROWS, ROWS, HALF), BF16),
            pltpu.VMEM((ROWS * ROWS, HALF), F32),
            pltpu.VMEM((3, 2, SHOTS, QUADS, ROWS, QUAD * HALF), BF16),
            pltpu.VMEM((3, NZ, QUAD * HALF), BF16),
            pltpu.VMEM((3, NZ, NZ), BF16),
            pltpu.VMEM((3, SLABS, ROWS, QUAD * HALF), BF16),
            pltpu.VMEM((2, QUADS, 3, ROWS, QUAD * HALF), BF16),
            pltpu.VMEM((3, ROWS * ROWS, HALF), F32),
            pltpu.VMEM((2, ROWS, ROWS, wide), F32),
            pltpu.VMEM((2, 3, (ROWS + 2) * ROWS, HALF), F32),
            pltpu.VMEM((2, 3, ROWS, wide), F32),
            pltpu.VMEM((2, 2, 8, wide), F32),
            pltpu.VMEM((2, 3, 2 * ROWS, wide), F32),
            pltpu.VMEM((2, 2, 8, wide), F32),
            pltpu.VMEM((2, 3, ROWS, wide), F32),
            pltpu.SemaphoreType.REGULAR,
            pltpu.SemaphoreType.DMA((5,)),
            pltpu.SemaphoreType.DMA((3,)),
            pltpu.SemaphoreType.DMA((3,)),
            pltpu.SemaphoreType.DMA,
            pltpu.SemaphoreType.DMA((PIECES,)),
            pltpu.SemaphoreType.DMA,
            pltpu.SemaphoreType.DMA((3,)),
            pltpu.SemaphoreType.DMA,
            pltpu.SemaphoreType.DMA,
            pltpu.SemaphoreType.DMA((8,)),
            pltpu.SemaphoreType.DMA((8,)),
        ],
        compiler_params=pltpu.CompilerParams(
            collective_id=0, has_side_effects=True, vmem_limit_bytes=60 * 1024 * 1024
        ),
    )(partial_grads[0], model, tilt, widths, step_length)


def solution(mesh):
    placed = (
        P("shot", None, "slab", None, None),
        P(None, "slab", "shot", None),
        P("slab", "shot", None),
        P(),
        P(),
    )
    return jax.shard_map(
        shards, mesh=mesh, in_specs=placed, out_specs=P(None, "slab", "shot", None), check_vma=False
    )
```

time: 123 us -> 126 us (1.024)
  the two profiles are of different devices: /device:TPU:6 before, /device:TPU:98 now
where the time goes in v4:
time: 126 us
  Pallas kernels  124 us (98%)
  local copies, waits for them, and re-layouts  2.06 us (2%)
    pallas_call x1, Pallas kernels, shards(): pl.pallas_call(kernel, out_shape=jax.ShapeDtypeStruct(model.shape, F32),...  124 us

profile of v4, /device:TPU:98, one launch (start us, length us, event | category | flops | bytes accessed | tf_op | source)
XLA Modules:
  0.0 125.6 jit_solution(16212476862389715362)
XLA Ops:
  0.0 123.6 %shard_map.55 = f32[3,16,16,256]{3,2,1,0:T(8,128)} custom-call(bf16[3,16,128,256]{3,2,1,0:T(8,128)(2,1)} %bitcast.1, f32[3,16,16,256]{3,2,1,0:T(8,128)} %model_hbm.1, f32[16,16,256]{2,1,0:T(8,128)} %tilt_hbm.1, f32[3,1024]{1,0:T(4,128)} %widths_hbm.1, f32[3]{0:T(128)} %step_hbm.1), custom_call_target="tpu_custom_call" | custom-call | tf_op jit(solution)/shard_map/pallas_call | solution.py:429
  123.6 2.1 %copy.7 = f32[3,16,16,256]{3,2,1,0:T(8,128)} copy(f32[3,16,16,256]{3,2,1,0:T(8,128)} %shard_map.55) | data formatting | bytes 1572864

commit v5 on v3

--- a/solution.py
+++ b/solution.py
@@ -193,7 +193,7 @@
             product[p, pl.ds(d0, BLOCK // ROWS)] = value.astype(BF16).reshape(BLOCK // ROWS, ROWS, 2 * HALF)
 
             def to_slab(i, inner):
-                d = d0 + (i + slab) % (BLOCK // ROWS)
+                d = d0 + (i + upper) % 2 * 8 + (i // 2 + slab) % 8
                 here = (d == slab) & (chunk_own == shot)
 
                 @pl.when(jnp.logical_not(here))
@@ -286,40 +286,40 @@
     pltpu.make_async_copy(back, back, back_recv).wait()
 
     for h in range(2):
-        ys = slice(h * HALF, (h + 1) * HALF)
         for p in range(3):
             for j in range(8):
                 for i in range(2):
                     x = 2 * j + i
-                    flat[p, x * ROWS : (x + 1) * ROWS, :] = back[h, j, p, :, i * HALF : (i + 1) * HALF].astype(F32)
-
-        def update(z, carry):
-            new = [
-                model[p, z, :, ys] - step[p] * flat[p, pl.ds(z, ROWS, stride=ROWS), :]
-                for p in range(3)
-            ]
-            squared = new[0] * new[0]
-            along = squared * (1.0 + 2.0 * new[1])
-            normal = squared * (1.0 + 2.0 * new[2])
-            cosine = wave[0, z, :, ys]
-            sine = wave[1, z, :, ys]
-            cc = cosine * cosine
-            ss = sine * sine
-            values = (along * cc + squared * ss, along * ss + squared * cc, (normal - squared) * (sine * cosine))
-            for n in range(3):
-                r0 = pl.multiple_of((z + 1) * ROWS, ROWS)
-                rot[h, n, pl.ds(r0, ROWS), :] = values[n]
-            return carry
-
-        lax.fori_loop(0, ROWS, update, 0)
+                    flat[h, p, x * ROWS : (x + 1) * ROWS, :] = back[h, j, p, :, i * HALF : (i + 1) * HALF].astype(F32)
+
+    def update(z, h):
+        ys = slice(h * HALF, (h + 1) * HALF)
+        new = [
+            model[p, z, :, ys] - step[p] * flat[h, p, pl.ds(z, ROWS, stride=ROWS), :]
+            for p in range(3)
+        ]
+        squared = new[0] * new[0]
+        along = squared * (1.0 + 2.0 * new[1])
+        normal = squared * (1.0 + 2.0 * new[2])
+        cosine = wave[0, z, :, ys]
+        sine = wave[1, z, :, ys]
+        cc = cosine * cosine
+        ss = sine * sine
+        values = (along * cc + squared * ss, along * ss + squared * cc, (normal - squared) * (sine * cosine))
+        r0 = (z + 1) * ROWS
+        if not isinstance(z, int):
+            r0 = pl.multiple_of(r0, ROWS)
         for n in range(3):
-            border[0, n, :, ys] = rot[h, n, pl.ds(ROWS, ROWS, stride=ROWS), :]
-            border[1, n, :, ys] = rot[h, n, pl.ds(2 * ROWS - 1, ROWS, stride=ROWS), :]
-
-    for s in range(2):
-        for n in range(3):
-            corner[s, 0, n : n + 1, :] = border[s, n, 0:1, :]
-            corner[s, 1, n : n + 1, :] = border[s, n, ROWS - 1 : ROWS, :]
+            rot[h, n, pl.ds(r0, ROWS), :] = values[n]
+
+    for h in range(2):
+        ys = slice(h * HALF, (h + 1) * HALF)
+        for zs, z in enumerate((0, ROWS - 1)):
+            update(z, h)
+            for xs, x in enumerate((0, ROWS - 1)):
+                r0 = (z + 1) * ROWS + x
+                for n in range(3):
+                    corner[xs, zs, n : n + 1, ys] = rot[h, n, r0 : r0 + 1, :]
 
     moves = []
     for index, (dx, dz) in enumerate(
@@ -345,9 +345,28 @@
         moves.append((copy, goes, comes, target, dx, dz))
 
     for copy, goes, comes, target, dx, dz in moves:
-        @pl.when(goes)
-        def _():
-            copy.start()
+        if dz != 0:
+            @pl.when(goes)
+            def _():
+                copy.start()
+
+    def update_both(z, carry):
+        update(z, 0)
+        update(z, 1)
+        return carry
+
+    lax.fori_loop(1, ROWS - 1, update_both, 0)
+    for h in range(2):
+        ys = slice(h * HALF, (h + 1) * HALF)
+        for n in range(3):
+            border[0, n, :, ys] = rot[h, n, pl.ds(ROWS, ROWS, stride=ROWS), :]
+            border[1, n, :, ys] = rot[h, n, pl.ds(2 * ROWS - 1, ROWS, stride=ROWS), :]
+
+    for copy, goes, comes, target, dx, dz in moves:
+        if dz == 0:
+            @pl.when(goes)
+            def _():
+                copy.start()
 
         if dx != 0:
             @pl.when(jnp.logical_not(comes))
@@ -434,7 +453,7 @@
             pltpu.VMEM((3, NZ, NZ), BF16),
             pltpu.VMEM((3, SLABS, ROWS, wide), BF16),
             pltpu.VMEM((2, 8, 3, ROWS, wide), BF16),
-            pltpu.VMEM((3, ROWS * ROWS, HALF), F32),
+            pltpu.VMEM((2, 3, ROWS * ROWS, HALF), F32),
             pltpu.VMEM((2, ROWS, ROWS, wide), F32),
             pltpu.VMEM((2, 3, (ROWS + 2) * ROWS, HALF), F32),
             pltpu.VMEM((2, 3, ROWS, wide), F32),

time: 110 us -> 109 us (level); the launches traced: 110 us -> 107 us
  Pallas kernels: 108 us -> 105 us
    pallas_call x1, Pallas kernels: 108 us -> 105 us  [shards(): pl.pallas_call(kernel, out_shape=jax.ShapeDtypeStruct(model.shape, F32),...]
where the time goes in v5:
time: 109 us; the launch traced here: 107 us
  Pallas kernels  105 us (96%)
  local copies, waits for them, and re-layouts  2.06 us (2%)
    pallas_call x1, Pallas kernels, shards(): pl.pallas_call(kernel, out_shape=jax.ShapeDtypeStruct(model.shape, F32),...  105 us

profile of v5, /device:TPU:6, one launch (start us, length us, event | category | flops | bytes accessed | tf_op | source)
XLA Modules:
  0.0 107.2 jit_solution(6465705418026730032)
XLA Ops:
  0.0 105.1 %shard_map.55 = f32[3,16,16,256]{3,2,1,0:T(8,128)} custom-call(bf16[3,16,128,256]{3,2,1,0:T(8,128)(2,1)} %bitcast.1, f32[3,16,16,256]{3,2,1,0:T(8,128)} %model_hbm.1, f32[16,16,256]{2,1,0:T(8,128)} %tilt_hbm.1, f32[3,1024]{1,0:T(4,128)} %widths_hbm.1, f32[3]{0:T(128)} %step_hbm.1), custom_call_target="tpu_custom_call" | custom-call | tf_op jit(solution)/shard_map/pallas_call | solution.py:438
  105.1 2.1 %copy.7 = f32[3,16,16,256]{3,2,1,0:T(8,128)} copy(f32[3,16,16,256]{3,2,1,0:T(8,128)} %shard_map.55) | data formatting | bytes 1572864

commit v6 on v5

--- a/solution.py
+++ b/solution.py
@@ -200,14 +200,14 @@
                 def _():
                     pltpu.make_async_remote_copy(
                         src_ref=product.at[p, d], dst_ref=back.at[end_half, pair_own, p],
-                        send_sem=back_send, recv_sem=back_recv,
+                        send_sem=back_send, recv_sem=back_recv.at[p],
                         device_id={"shot": chunk_own, "slab": d}, device_id_type=MESH,
                     ).start()
 
                 @pl.when(here)
                 def _():
                     pltpu.make_async_copy(
-                        product.at[p, d], back.at[end_half, pair_own, p], back_recv
+                        product.at[p, d], back.at[end_half, pair_own, p], back_recv.at[p]
                     ).start()
 
                 return inner
@@ -283,10 +283,10 @@
 
     lax.fori_loop(0, ROWS, waves, 0)
 
-    pltpu.make_async_copy(back, back, back_recv).wait()
-
-    for h in range(2):
-        for p in range(3):
+    for p in range(3):
+        landed = back.at[:, :, p]
+        pltpu.make_async_copy(landed, landed, back_recv.at[p]).wait()
+        for h in range(2):
             for j in range(8):
                 for i in range(2):
                     x = 2 * j + i
@@ -468,7 +468,7 @@
             pltpu.SemaphoreType.DMA,
             pltpu.SemaphoreType.DMA((3,)),
             pltpu.SemaphoreType.DMA,
-            pltpu.SemaphoreType.DMA,
+            pltpu.SemaphoreType.DMA((3,)),
             pltpu.SemaphoreType.DMA((8,)),
             pltpu.SemaphoreType.DMA((8,)),
         ],

time: 109 us -> 109 us (level)
  no operation moved by 1% of the time
where the time goes in v6:
time: 109 us; the launch traced here: 107 us
  Pallas kernels  105 us (96%)
  local copies, waits for them, and re-layouts  2.06 us (2%)
    pallas_call x1, Pallas kernels, shards(): pl.pallas_call(kernel, out_shape=jax.ShapeDtypeStruct(model.shape, F32),...  105 us

profile of v6, /device:TPU:6, one launch (start us, length us, event | category | flops | bytes accessed | tf_op | source)
XLA Modules:
  0.0 107.2 jit_solution(18355986993731494934)
XLA Ops:
  0.0 105.1 %shard_map.55 = f32[3,16,16,256]{3,2,1,0:T(8,128)} custom-call(bf16[3,16,128,256]{3,2,1,0:T(8,128)(2,1)} %bitcast.1, f32[3,16,16,256]{3,2,1,0:T(8,128)} %model_hbm.1, f32[16,16,256]{2,1,0:T(8,128)} %tilt_hbm.1, f32[3,1024]{1,0:T(4,128)} %widths_hbm.1, f32[3]{0:T(128)} %step_hbm.1), custom_call_target="tpu_custom_call" | custom-call | tf_op jit(solution)/shard_map/pallas_call | solution.py:438
  105.1 2.1 %copy.7 = f32[3,16,16,256]{3,2,1,0:T(8,128)} copy(f32[3,16,16,256]{3,2,1,0:T(8,128)} %shard_map.55) | data formatting | bytes 1572864
